TPU v7x, 32 devices: a whole 2x2x4 slice. The times are simulated.
32 devices in a mesh: groups: 2 (over x), tensor: 16 (over z, y, core).
Axes of the slice: x: 2, y: 2, z: 4, core: 2. Of those that a mesh axis runs over, the one named last changes fastest.
Arguments:
- tokens: bfloat16 [1024, 2560], P(('groups', 'tensor')), parts along dimension 0, may hold values from -6 to 6
- grad_out: bfloat16 [1024, 2560], P(('groups', 'tensor')), parts along dimension 0, may hold values from -6 to 6
- gate_base: bfloat16 [2560, 13824], P(None, 'tensor'), may hold values from -0.125 to 0.125
- up_base: bfloat16 [2560, 13824], P(None, 'tensor'), may hold values from -0.125 to 0.125
- down_base: bfloat16 [13824, 2560], P('tensor'), may hold values from -0.0546875 to 0.0546875
- gate_delta: bfloat16 [2, 2560, 13824], P(None, None, 'tensor'), may hold values from -0.03125 to 0.03125
- up_delta: bfloat16 [2, 2560, 13824], P(None, None, 'tensor'), may hold values from -0.03125 to 0.03125
- down_delta: bfloat16 [2, 13824, 2560], P(None, 'tensor'), may hold values from -0.015625 to 0.015625
- offsets: int32 [3, 16], P(None, 'tensor'), may hold values from 0 to 1073741823
- seeds: int32 [4], P('groups'), parts along dimension 0, may hold values from 0 to 1073741823
Outputs:
- mixed: bfloat16 [1024, 2560], P(('groups', 'tensor')), parts along dimension 0
- grad_tokens: bfloat16 [1024, 2560], P(('groups', 'tensor')), parts along dimension 0
- grad_gate: bfloat16 [5120, 13824], P('groups', 'tensor'), parts along dimension 0
- grad_up: bfloat16 [5120, 13824], P('groups', 'tensor'), parts along dimension 0
- grad_down: bfloat16 [27648, 2560], P(('groups', 'tensor')), parts along dimension 0
There are 2 independent parts, one for each index of `groups`. A program takes and returns all parts, laid end to end along the dimension named above; an argument that names none is the same for every part. Nothing has to cross between parts.
All inputs are finite; a program needn't handle non-finite values.
Results may differ from a plain program's by a relative error of at most 0.0061.
Values may be sent and summed in bfloat16 or wider, within the bound.
A program may use at most 192 MiB of HBM per device.

v0:
```python
import jax
import jax.numpy as jnp
from jax import lax
from jax.sharding import PartitionSpec as P


def shifted(value, amount):
    return lax.shift_right_logical(value, jnp.full_like(value, amount))


def kept_entries(number, seed_value):
    mixing = number * jnp.int32(-1640531535) + seed_value * jnp.int32(-2048144777)
    mixing = jnp.bitwise_xor(mixing, shifted(mixing, 15))
    mixing = mixing * jnp.int32(-1028477379)
    mixing = jnp.bitwise_xor(mixing, shifted(mixing, 13))
    mixing = mixing * jnp.int32(668265263)
    mixing = jnp.bitwise_xor(mixing, shifted(mixing, 16))
    return shifted(mixing, 8) % 10 == 0


def merge_shard(base, delta, first_number, seeds):
    shape_rows, shape_cols = base.shape
    row_ids = lax.broadcasted_iota(jnp.int32, (shape_rows, shape_cols), 0)
    col_ids = lax.broadcasted_iota(jnp.int32, (shape_rows, shape_cols), 1)
    number = first_number + row_ids * shape_cols + col_ids
    first = jnp.where(
        kept_entries(number, seeds[0]), delta[0].astype(jnp.float32), jnp.float32(0.0)
    )
    second = jnp.where(
        kept_entries(number, seeds[1]), delta[1].astype(jnp.float32), jnp.float32(0.0)
    )
    return (base.astype(jnp.float32) + 5.0 * (first + second)).astype(jnp.bfloat16)


def per_device(
    tokens,
    grad_out,
    gate_base,
    up_base,
    down_base,
    gate_delta,
    up_delta,
    down_delta,
    offsets,
    seeds,
):
    gate_w = merge_shard(gate_base, gate_delta, offsets[0, 0], seeds)
    up_w = merge_shard(up_base, up_delta, offsets[1, 0], seeds)
    down_w = merge_shard(down_base, down_delta, offsets[2, 0], seeds)
    slab_cols = gate_w.shape[1]
    tok_all = lax.all_gather(tokens, "tensor", axis=0, tiled=True)
    pair_w = jnp.concatenate([gate_w, up_w], axis=1)
    projected = jnp.dot(tok_all, pair_w, preferred_element_type=jnp.float32)
    gate_pre = projected[:, :slab_cols]
    up_pre = projected[:, slab_cols:]
    sigmoid_gate = jax.nn.sigmoid(gate_pre)
    hidden = (gate_pre * sigmoid_gate * up_pre).astype(jnp.bfloat16)
    rows_block = hidden
    mixed = lax.psum_scatter(
        jnp.dot(rows_block, down_w, preferred_element_type=jnp.float32),
        "tensor",
        scatter_dimension=0,
        tiled=True,
    ).astype(jnp.bfloat16)
    grad_all = lax.all_gather(grad_out, "tensor", axis=0, tiled=True)
    grad_hidden = lax.dot_general(
        grad_all, down_w, (((1,), (1,)), ((), ())), preferred_element_type=jnp.float32
    )
    grad_gate_act = (
        grad_hidden * up_pre * sigmoid_gate * (1.0 + gate_pre * (1.0 - sigmoid_gate))
    ).astype(jnp.bfloat16)
    grad_up_act = (grad_hidden * gate_pre * sigmoid_gate).astype(jnp.bfloat16)
    grad_down = lax.dot_general(
        hidden, grad_all, (((0,), (0,)), ((), ())), preferred_element_type=jnp.float32
    ).astype(jnp.bfloat16)
    grad_pair_act = jnp.concatenate([grad_gate_act, grad_up_act], axis=1)
    grad_pair = lax.dot_general(
        tok_all, grad_pair_act, (((0,), (0,)), ((), ())), preferred_element_type=jnp.float32
    ).astype(jnp.bfloat16)
    rows_block = grad_pair_act
    grad_tokens = lax.psum_scatter(
        lax.dot_general(
            rows_block, pair_w, (((1,), (1,)), ((), ())), preferred_element_type=jnp.float32
        ),
        "tensor",
        scatter_dimension=0,
        tiled=True,
    ).astype(jnp.bfloat16)
    return (mixed, grad_tokens, grad_pair[:, :slab_cols], grad_pair[:, slab_cols:], grad_down)


def solution(mesh):
    placed = (
        P(("groups", "tensor"), None),
        P(("groups", "tensor"), None),
        P(None, "tensor"),
        P(None, "tensor"),
        P("tensor", None),
        P(None, None, "tensor"),
        P(None, None, "tensor"),
        P(None, "tensor", None),
        P(None, "tensor"),
        P("groups"),
    )
    return jax.shard_map(
        per_device,
        mesh=mesh,
        in_specs=placed,
        out_specs=(
            P(("groups", "tensor"), None),
            P(("groups", "tensor"), None),
            P("groups", "tensor"),
            P("groups", "tensor"),
            P(("groups", "tensor"), None),
        ),
        check_vma=False,
    )
```

profile of v0, /device:TPU:0, one launch (start us, length us, event | category | flops | bytes accessed | tf_op | source)
XLA Modules:
  0.0 282.4 jit_solution(6615076492970896005)
XLA Ops:
  7.2 0.0 all-gather.3.cloned.1.call-start
  7.2 0.0 slice-start
  7.2 0.7 all-gather.3.cloned.1.call-update
  7.9 0.0 all-gather.5.cloned.1.call-start
  7.9 0.7 all-gather.5.cloned.1.call-update
  8.6 0.0 reduce-scatter.5.cloned.1.call-start
  8.7 1.3 fusion.58
  11.3 1.4 fusion.57
  12.7 0.6 multiply_add_fusion
  13.3 0.7 fusion.52
  14.0 0.7 fusion.51
  14.6 0.0 slice-start.1
  14.6 0.0 slice-start.2
  14.7 0.0 copy-start
  14.7 40.4 %fusion.38 = (bf16[2560,864]{0,1:T(8,128)(2,1)}, bf16[2560,864]{0,1:T(8,128)(2,1)}) fusion(bf16[2560,864]{0,1:T(8,128)(2,1)} %param.13, bf16[2,2560,864]{1,2,0:T(8,128)(2,1)} %param.16, s32[2560]{0:T(1024)S(1)} %fusion.51, s32[]{:T(128)} %bitcast.3, s32[]{:T(128)} %bitcast.1, bf16[2,2560,864]{1,2,0:T(8,128)(2,1)} %param.15, s32[2560]{0:T(1024)S(1)} %fusion.52, ...), kind=kLoop, calls=%fused_computation.67 | loop fusion | flops 199065600 | bytes 35409928 | tf_op jit(solution)/shard_map/convert_element_type | solution.py:32
  55.1 0.0 slice-done
  55.1 0.0 slice-done.1
  55.1 0.0 slice-done.2
  55.1 0.0 copy-done
  55.1 20.3 %fusion.34 = bf16[864,2560]{1,0:T(8,128)(2,1)} fusion(bf16[864,2560]{1,0:T(8,128)(2,1)S(1)} %copy-done, bf16[2,864,2560]{2,1,0:T(8,128)(2,1)S(1)} %bitcast.49, s32[]{:T(128)} %bitcast.3, s32[]{:T(128)} %bitcast.1, s32[864]{0:T(1024)S(1)} %multiply_add_fusion), kind=kLoop, calls=%fused_computation.61 | loop fusion | flops 99532800 | bytes 17698184 | tf_op jit(solution)/shard_map/convert_element_type | solution.py:32
  75.4 0.0 all-gather.3.cloned.1.call-done
  75.4 10.9 %fusion.45 = f32[512,1728]{0,1:T(8,128)} fusion(bf16[512,2560]{1,0:T(8,128)(2,1)} %all-gather.3.cloned.1.call-done, bf16[2560,864]{0,1:T(8,128)(2,1)} %get-tuple-element.15, bf16[2560,864]{0,1:T(8,128)(2,1)} %get-tuple-element.16), kind=kOutput, calls=%fused_computation.81 | convolution fusion | flops 4547543040 | bytes 15007744 | tf_op jit(solution)/shard_map/dot_general | solution.py:53
  86.3 14.1 %all-gather.5.cloned.1.call-done = bf16[512,2560]{1,0:T(8,128)(2,1)} async-done(((bf16[32,2560]{1,0:T(8,128)(2,1)}), bf16[512,2560]{1,0:T(8,128)(2,1)}) %all-gather.5.cloned.1.call-update) | async-done | bytes 2621456 | tf_op jit(solution)/shard_map/all_gather | solution.py:65
  100.3 0.0 copy-start.1
  100.3 0.0 copy-start.2
  100.4 7.3 %fusion.48 = (bf16[512,864]{0,1:T(8,128)(2,1)S(1)}, bf16[512,864]{0,1:T(8,128)(2,1)S(1)}, bf16[512,864]{0,1:T(8,128)(2,1)S(1)}) fusion(f32[512,1728]{0,1:T(8,128)} %fusion.45, bf16[864,2560]{1,0:T(8,128)(2,1)} %fusion.34, bf16[512,2560]{1,0:T(8,128)(2,1)} %all-gather.5.cloned.1.call-done), kind=kOutput, calls=%fused_computation.87 | convolution fusion | flops 2272002048 | bytes 13238272 | tf_op jit(solution)/shard_map/dot_general | solution.py:66
  107.7 0.0 copy-start.5
  107.7 0.0 copy-start.7
  107.7 0.9 copy-done.5
  108.6 0.3 copy-done.7
  108.9 0.0 copy-done.1
  108.9 0.0 copy-done.2
  108.9 6.9 %fusion.43 = f32[512,2560]{1,0:T(8,128)} fusion(bf16[2560,864]{0,1:T(8,128)(2,1)S(1)} %copy-done.1, bf16[2560,864]{0,1:T(8,128)(2,1)S(1)} %copy-done.2, bf16[512,864]{0,1:T(8,128)(2,1)S(1)} %get-tuple-element.8, bf16[512,864]{0,1:T(8,128)(2,1)S(1)} %get-tuple-element.7), kind=kOutput, calls=%fused_computation.78 | convolution fusion | flops 4551081984 | bytes 15859712 | tf_op jit(solution)/shard_map/dot_general | solution.py:82
  115.8 0.0 reduce-scatter.5.cloned.1.call-update
  115.9 0.0 copy-start.4
  115.9 0.2 reduce-scatter.3.cloned.1.call-start
  116.1 7.1 %fusion.59 = f32[512,2560]{1,0:T(8,128)} fusion(bf16[512,864]{0,1:T(8,128)(2,1)S(1)} %get-tuple-element.9, bf16[864,2560]{1,0:T(8,128)(2,1)} %fusion.34), kind=kOutput, calls=%fused_computation.102 | convolution fusion | flops 2264924160 | bytes 10551296 | tf_op jit(solution)/shard_map/dot_general | solution.py:60
  123.2 0.0 reduce-scatter.3.cloned.1.call-update
  123.2 0.0 copy-done.4
  123.2 0.0 copy-start.3
  123.2 0.0 copy-start.6
  123.2 0.0 copy-start.8
  123.2 4.5 %convolution_convert_fusion.1 = bf16[864,2560]{1,0:T(8,128)(2,1)} fusion(bf16[512,864]{0,1:T(8,128)(2,1)S(1)} %get-tuple-element.9, bf16[512,2560]{1,0:T(8,128)(2,1)S(1)} %copy-done.4), kind=kOutput, calls=%fused_computation.80 | convolution fusion | flops 2267136000 | bytes 7929856 | tf_op jit(solution)/shard_map/dot_general | solution.py:73
  127.8 0.0 copy-done.3
  127.8 0.0 copy-done.6
  127.8 0.0 copy-done.8
  127.8 6.2 %fusion = bf16[2560,1728]{0,1:T(8,128)(2,1)S(1)} fusion(bf16[512,2560]{1,0:T(8,128)(2,1)S(1)} %copy-done.3, bf16[512,864]{0,1:T(8,128)(2,1)S(1)} %copy-done.8, bf16[512,864]{0,1:T(8,128)(2,1)S(1)} %copy-done.6), kind=kOutput, calls=%fused_computation.25 | convolution fusion | flops 4537810944 | bytes 13238272 | tf_op jit(solution)/shard_map/dot_general | solution.py:77
  134.0 3.8 %fusion.56 = (bf16[2560,864]{0,1:T(8,128)(2,1)}, bf16[2560,864]{0,1:T(8,128)(2,1)}) fusion(bf16[2560,1728]{0,1:T(8,128)(2,1)S(1)} %fusion), kind=kLoop, calls=%fused_computation.99 | loop fusion | bytes 17694720 | tf_op jit(solution)/shard_map/slice | solution.py:89
  137.8 55.3 %reduce-scatter.5.cloned.1.call-done = f32[32,2560]{1,0:T(8,128)} async-done(((f32[512,2560]{1,0:T(8,128)}), f32[32,2560]{1,0:T(8,128)}) %reduce-scatter.5.cloned.1.call-update) | async-done | bytes 327696 | tf_op jit(solution)/shard_map/reduce_scatter | solution.py:81
  193.1 1.7 convert_element_type.100
  194.8 79.5 %reduce-scatter.3.cloned.1.call-done = f32[32,2560]{1,0:T(8,128)} async-done(((f32[512,2560]{1,0:T(8,128)}), f32[32,2560]{1,0:T(8,128)}) %reduce-scatter.3.cloned.1.call-update) | async-done | bytes 327696 | tf_op jit(solution)/shard_map/reduce_scatter | solution.py:59
  274.2 1.7 convert_element_type.97
  (1 shorter events, 0.0 us)
Async XLA Ops:
  7.2 68.2 %all-gather.3.cloned.1.call-start = ((), (), s32[]{:S(2)}) async-start(), calls=%async_computation.2 | async-start | bytes 2785280 | tf_op jit(solution)/shard_map/all_gather | solution.py:51
  7.2 47.9 %slice-start = ((s8[8847360]{0:T(1024)(128)(4,1)}), s8[458752]{0:T(1024)(128)(4,1)S(1)}, s32[]{:S(2)}) async-start(s8[8847360]{0:T(1024)(128)(4,1)} %bitcast.48), calls=%async_computation.6 | async-start | bytes 917504
  7.9 92.4 %all-gather.5.cloned.1.call-start = ((), (), s32[]{:S(2)}) async-start(), calls=%async_computation.4 | async-start | bytes 2785280 | tf_op jit(solution)/shard_map/all_gather | solution.py:65
  8.6 184.5 %reduce-scatter.5.cloned.1.call-start = ((), (), s32[]{:S(2)}) async-start(), calls=%async_computation.5 | async-start | bytes 5570560 | tf_op jit(solution)/shard_map/reduce_scatter | solution.py:81
  14.6 40.4 %slice-start.1 = ((s8[8847360]{0:T(1024)(128)(4,1)}), s8[4194304]{0:T(1024)(128)(4,1)S(1)}, s32[]{:S(2)}) async-start(s8[8847360]{0:T(1024)(128)(4,1)} %bitcast.48), calls=%async_computation.7 | async-start | bytes 8388608
  14.6 40.4 %slice-start.2 = ((s8[8847360]{0:T(1024)(128)(4,1)}), s8[4194304]{0:T(1024)(128)(4,1)S(1)}, s32[]{:S(2)}) async-start(s8[8847360]{0:T(1024)(128)(4,1)} %bitcast.48), calls=%async_computation.8 | async-start | bytes 8388608
  14.7 40.4 %copy-start = (bf16[864,2560]{1,0:T(8,128)(2,1)S(1)}, bf16[864,2560]{1,0:T(8,128)(2,1)}, u32[]{:S(2)}) copy-start(bf16[864,2560]{1,0:T(8,128)(2,1)} %param.14) | copy-start | bytes 13271044
  100.3 8.6 %copy-start.1 = (bf16[2560,864]{0,1:T(8,128)(2,1)S(1)}, bf16[2560,864]{0,1:T(8,128)(2,1)}, u32[]{:S(2)}) copy-start(bf16[2560,864]{0,1:T(8,128)(2,1)} %get-tuple-element.15) | copy-start | bytes 13271044
  100.3 8.6 %copy-start.2 = (bf16[2560,864]{0,1:T(8,128)(2,1)S(1)}, bf16[2560,864]{0,1:T(8,128)(2,1)}, u32[]{:S(2)}) copy-start(bf16[2560,864]{0,1:T(8,128)(2,1)} %get-tuple-element.16) | copy-start | bytes 13271044
  107.7 0.9 copy-start.5
  107.7 1.2 copy-start.7
  115.9 7.3 %copy-start.4 = (bf16[512,2560]{1,0:T(8,128)(2,1)S(1)}, bf16[512,2560]{1,0:T(8,128)(2,1)}, u32[]{:S(2)}) copy-start(bf16[512,2560]{1,0:T(8,128)(2,1)} %all-gather.5.cloned.1.call-done) | copy-start | bytes 7864324
  115.9 158.4 %reduce-scatter.3.cloned.1.call-start = ((), (), s32[]{:S(2)}) async-start(), calls=%async_computation.3 | async-start | bytes 5570560 | tf_op jit(solution)/shard_map/reduce_scatter | solution.py:59
  123.2 4.6 %copy-start.3 = (bf16[512,2560]{1,0:T(8,128)(2,1)S(1)}, bf16[512,2560]{1,0:T(8,128)(2,1)}, u32[]{:S(2)}) copy-start(bf16[512,2560]{1,0:T(8,128)(2,1)} %all-gather.3.cloned.1.call-done) | copy-start | bytes 7864324
  123.2 4.6 %copy-start.6 = (bf16[512,864]{0,1:T(8,128)(2,1)S(1)}, bf16[512,864]{0,1:T(8,128)(2,1)}, u32[]{:S(2)}) copy-start(bf16[512,864]{0,1:T(8,128)(2,1)} %copy-done.5) | copy-start | bytes 2654212
  123.2 4.6 %copy-start.8 = (bf16[512,864]{0,1:T(8,128)(2,1)S(1)}, bf16[512,864]{0,1:T(8,128)(2,1)}, u32[]{:S(2)}) copy-start(bf16[512,864]{0,1:T(8,128)(2,1)} %copy-done.7) | copy-start | bytes 2654212
Sparse Core Ops, SparseCore 0:
  10.3 45.9 all-gather.2
  58.5 41.7 all-gather.4
  116.0 77.0 reduce-scatter.4
  196.8 77.3 reduce-scatter.2
where the time goes:
time: 283 us; the launch traced here: 282 us
  waiting for transfers between devices  150 us (53%)
  other arithmetic  65.9 us (23%)
  matrix products  43 us (15%)
  between operations  15.2 us (5%)
  local copies, waits for them, and re-layouts  7.71 us (3%)
    reduce_scatter x1, waiting for transfers between devices, per_device(): lax.psum_scatter(jnp.dot(rows_block, down_w, preferred_element_type=jnp.f...  79.5 us
    convert_element_type x2, other arithmetic, merge_shard(): (base.astype(jnp.float32) + 5.0 * (first + second)).astype(jnp.bfloat16)  60.7 us
    reduce_scatter x1, waiting for transfers between devices, per_device(): lax.psum_scatter(lax.dot_general(rows_block, pair_w, (((1,), (1,)), ((),...  55.3 us
    all_gather x1, waiting for transfers between devices, per_device(): grad_all = lax.all_gather(grad_out, 'tensor', axis=0, tiled=True)  14.1 us
    dot_general x1, matrix products, per_device(): projected = jnp.dot(tok_all, pair_w, preferred_element_type=jnp.float32)  10.9 us
    dot_general x1, matrix products, per_device(): lax.dot_general(grad_all, down_w, (((1,), (1,)), ((), ())), preferred_ele...  7.32 us
    dot_general x1, matrix products, per_device(): jnp.dot(rows_block, down_w, preferred_element_type=jnp.float32)  7.08 us
    dot_general x1, matrix products, per_device(): lax.dot_general(rows_block, pair_w, (((1,), (1,)), ((), ())), preferred_e...  6.93 us
  transfers between devices with their start and end apart: 4, of which 3 were waited for; matrix products, arithmetic and copies ran while one was open for 35% of the time, Pallas kernels for 0%

commit v1 on v0

v1 whole, which is shorter than its diff:
```python
import functools

import jax
import jax.numpy as jnp
from jax import lax
from jax.experimental import pallas as pl
from jax.experimental.pallas import tpu as pltpu
from jax.sharding import PartitionSpec as P

MESH = pl.DeviceIdType.MESH
MUL_I = -1640531535
MUL_S = -2048144777
TENTH = 429496730
LOW = -(1 << 31)
COLS = 128


def srl(value, amount):
    return lax.shift_right_logical(value, jnp.full_like(value, amount))


def kept(mix):
    mix = mix ^ srl(mix, 15)
    mix = mix * jnp.int32(-1028477379)
    mix = mix ^ srl(mix, 13)
    mix = mix * jnp.int32(668265263)
    mix = mix ^ srl(mix, 16)
    scaled = srl(mix, 8) * jnp.int32(TENTH)
    return (scaled ^ jnp.int32(LOW)) < jnp.int32(TENTH + LOW)


def merge_block(base, delta, out, row_mul, col_mul, start0, start1):
    rows = base.shape[0]
    chunk = next((c for c in (96, 48, 32, 16) if rows % c == 0), rows)
    row_ids = lax.broadcasted_iota(jnp.int32, (chunk, COLS), 0)
    col_ids = lax.broadcasted_iota(jnp.int32, (chunk, COLS), 1)
    ids = row_ids * jnp.int32(row_mul) + col_ids * jnp.int32(col_mul)

    def piece(sel, shift):
        first = jnp.where(kept(ids + (start0 + shift)), delta[0, sel, :].astype(jnp.float32), 0.0)
        second = jnp.where(kept(ids + (start1 + shift)), delta[1, sel, :].astype(jnp.float32), 0.0)
        merged = base[sel, :].astype(jnp.float32) + 5.0 * (first + second)
        out[sel, :] = merged.astype(jnp.bfloat16)

    if chunk == rows:
        piece(slice(None), jnp.int32(0))
    else:
        @pl.loop(0, rows // chunk)
        def _(i):
            piece(pl.ds(pl.multiple_of(i * chunk, chunk), chunk), i * jnp.int32(wrap(chunk * row_mul)))


def wrap(value):
    return (value + (1 << 31)) % (1 << 32) - (1 << 31)


def place(n):
    me = lax.axis_index("tensor")
    return lax.div(me, 4), lax.rem(lax.div(me, 2), 2), lax.rem(me, 2)


def merge_kernel(
    n, offs, seeds, tok, grd, gb, ub, db, gd, ud, dd,
    gw, uw, dw, tok_all, grd_all,
    loc_sem, zs, zr, ys, yr, cs, cr,
):
    nz = n // 4
    step = pl.program_id(0)
    last = tok.shape[1] // COLS - 1
    z, y, c = place(n)
    ins, outs = (tok, grd), (tok_all, grd_all)

    def index(zz, yy, cc):
        return {"tensor": (zz * 2 + yy) * 2 + cc}

    def local(a):
        return pltpu.make_async_copy(ins[a], outs[a].at[z, y, c], loc_sem.at[a])

    def z_send(a, d):
        return pltpu.make_async_remote_copy(
            src_ref=ins[a], dst_ref=outs[a].at[z, y, c], send_sem=zs.at[a, d - 1], recv_sem=zr.at[a, d - 1],
            device_id=index(lax.rem(z + d, nz), y, c), device_id_type=MESH)

    def z_recv(a, d):
        return pltpu.make_async_remote_copy(
            src_ref=ins[a], dst_ref=outs[a].at[lax.rem(z + nz - d, nz), y, c], send_sem=zs.at[a, d - 1],
            recv_sem=zr.at[a, d - 1], device_id=index(lax.rem(z + d, nz), y, c), device_id_type=MESH)

    def y_copy(a, d):
        zz = lax.rem(z + nz - d, nz)
        block = outs[a].at[zz, y, c]
        return pltpu.make_async_remote_copy(
            src_ref=ins[a] if d == 0 else block, dst_ref=block, send_sem=ys.at[a, d], recv_sem=yr.at[a, d],
            device_id=index(z, 1 - y, c), device_id_type=MESH)

    def y_recv(a, d):
        block = outs[a].at[lax.rem(z + nz - d, nz), 1 - y, c]
        return pltpu.make_async_remote_copy(
            src_ref=ins[a], dst_ref=block, send_sem=ys.at[a, d], recv_sem=yr.at[a, d],
            device_id=index(z, 1 - y, c), device_id_type=MESH)

    def c_copy(a):
        part = outs[a].at[:, :, c]
        return pltpu.make_async_remote_copy(
            src_ref=part, dst_ref=part, send_sem=cs.at[a], recv_sem=cr.at[a],
            device_id=index(z, y, 1 - c), device_id_type=MESH)

    def c_recv(a):
        part = outs[a].at[:, :, 1 - c]
        return pltpu.make_async_remote_copy(
            src_ref=part, dst_ref=part, send_sem=cs.at[a], recv_sem=cr.at[a],
            device_id=index(z, y, 1 - c), device_id_type=MESH)

    @pl.when(step == 0)
    def _():
        barrier = pltpu.get_barrier_semaphore()
        for d in range(1, nz):
            pl.semaphore_signal(barrier, inc=1, device_id=index(lax.rem(z + d, nz), y, c), device_id_type=MESH)
        pl.semaphore_signal(barrier, inc=1, device_id=index(z, 1 - y, c), device_id_type=MESH)
        pl.semaphore_signal(barrier, inc=1, device_id=index(z, y, 1 - c), device_id_type=MESH)
        pl.semaphore_wait(barrier, nz + 1)
        for a in range(2):
            local(a).start()
            y_copy(a, 0).start()
            for d in range(1, nz):
                z_send(a, d).start()

    def forward_y(a):
        for d in range(1, nz):
            z_recv(a, d).wait_recv()
            y_copy(a, d).start()

    def forward_c(a):
        local(a).wait()
        for d in range(nz):
            y_recv(a, d).wait_recv()
        c_copy(a).start()

    @pl.when(step == last * 8 // 19)
    def _():
        forward_y(0)

    @pl.when(step == last * 14 // 19)
    def _():
        forward_c(0)

    @pl.when(step == last * 16 // 19)
    def _():
        forward_y(1)

    shard = gb.shape[0]
    seed0 = seeds[0] * jnp.int32(MUL_S)
    seed1 = seeds[1] * jnp.int32(MUL_S)
    for m, (base, delta, out) in enumerate(((gb, gd, gw), (ub, ud, uw), (db, dd, dw))):
        if m < 2:
            row_mul, col_mul = MUL_I, wrap(shard * MUL_I)
        else:
            row_mul, col_mul = wrap(tok.shape[1] * MUL_I), MUL_I
        first = offs[m] * jnp.int32(MUL_I) + step * jnp.int32(wrap(COLS * col_mul))
        merge_block(base, delta, out, row_mul, col_mul, first + seed0, first + seed1)

    @pl.when(step == last)
    def _():
        forward_c(1)
        for a in range(2):
            for d in range(1, nz):
                z_send(a, d).wait_send()
            for d in range(nz):
                y_copy(a, d).wait_send()
            c_copy(a).wait_send()
            c_recv(a).wait_recv()


def merge_and_gather(n, offs, seeds, tok, grd, gb, ub, db, gd, ud, dd):
    shard, width = gb.shape
    nz = n // 4
    plain = pl.BlockSpec((shard, COLS), lambda i: (0, i))
    pair = pl.BlockSpec((2, shard, COLS), lambda i: (0, 0, i))
    smem = pl.BlockSpec(memory_space=pltpu.SMEM)
    anyspace = pl.BlockSpec(memory_space=pl.ANY)
    weight = jax.ShapeDtypeStruct((shard, width), jnp.bfloat16)
    gathered = jax.ShapeDtypeStruct((nz, 2, 2) + tok.shape, tok.dtype)
    dma = pltpu.SemaphoreType.DMA
    return pl.pallas_call(
        functools.partial(merge_kernel, n),
        grid=(width // COLS,),
        in_specs=[smem, smem, anyspace, anyspace, plain, plain, plain, pair, pair, pair],
        out_specs=[plain, plain, plain, anyspace, anyspace],
        out_shape=[weight, weight, weight, gathered, gathered],
        scratch_shapes=[
            dma((2,)), dma((2, nz - 1)), dma((2, nz - 1)), dma((2, nz)), dma((2, nz)), dma((2,)), dma((2,)),
        ],
        compiler_params=pltpu.CompilerParams(
            collective_id=0, has_side_effects=True, vmem_limit_bytes=40 * 1024 * 1024,
            dimension_semantics=("arbitrary",)),
    )(offs, seeds, tok, grd, gb, ub, db, gd, ud, dd)


def scatter_kernel(
    n, parts, part0, part1, out0, out1,
    got_c, sum_c, got_y, sum_y, got_z, cs, cr, ys, yr, zs, zr,
):
    nz = n // 4
    z, y, c = place(n)
    width = out0.shape[1] // parts
    parts_in, outs = (part0, part1), (out0, out1)

    def index(zz, yy, cc):
        return {"tensor": (zz * 2 + yy) * 2 + cc}

    barrier = pltpu.get_barrier_semaphore()
    for d in range(1, nz):
        pl.semaphore_signal(barrier, inc=1, device_id=index(lax.rem(z + d, nz), y, c), device_id_type=MESH)
    pl.semaphore_signal(barrier, inc=1, device_id=index(z, 1 - y, c), device_id_type=MESH)
    pl.semaphore_signal(barrier, inc=1, device_id=index(z, y, 1 - c), device_id_type=MESH)
    pl.semaphore_wait(barrier, nz + 1)

    tasks = [(a, p) for a in range(2) for p in range(parts)]

    def c_copy(t):
        a, p = tasks[t]
        return pltpu.make_async_remote_copy(
            src_ref=parts_in[a].at[:, :, 1 - c, :, pl.ds(p * width, width)], dst_ref=got_c.at[t],
            send_sem=cs.at[t], recv_sem=cr.at[t], device_id=index(z, y, 1 - c), device_id_type=MESH)

    def y_copy(t):
        return pltpu.make_async_remote_copy(
            src_ref=sum_c.at[t, :, 1 - y], dst_ref=got_y.at[t],
            send_sem=ys.at[t], recv_sem=yr.at[t], device_id=index(z, 1 - y, c), device_id_type=MESH)

    def z_copy(t, d):
        zz = lax.rem(z + d, nz)
        return pltpu.make_async_remote_copy(
            src_ref=sum_y.at[t, zz], dst_ref=got_z.at[t, d - 1],
            send_sem=zs.at[t, d - 1], recv_sem=zr.at[t, d - 1], device_id=index(zz, y, c), device_id_type=MESH)

    for t in range(len(tasks)):
        c_copy(t).start()
    for t, (a, p) in enumerate(tasks):
        c_copy(t).wait_recv()

        @pl.loop(0, nz)
        def _(zz):
            for yy in range(2):
                mine = parts_in[a][zz, yy, c, :, pl.ds(p * width, width)].astype(jnp.float32)
                sum_c[t, zz, yy] = (mine + got_c[t, zz, yy].astype(jnp.float32)).astype(jnp.bfloat16)

        y_copy(t).start()
    for t in range(len(tasks)):
        y_copy(t).wait_recv()

        @pl.loop(0, nz)
        def _(zz):
            mine = sum_c[t, zz, y].astype(jnp.float32)
            sum_y[t, zz] = (mine + got_y[t, zz].astype(jnp.float32)).astype(jnp.bfloat16)

        for d in range(1, nz):
            z_copy(t, d).start()
    for t, (a, p) in enumerate(tasks):
        total = sum_y[t, z].astype(jnp.float32)
        for d in range(1, nz):
            z_copy(t, d).wait_recv()
            total = total + got_z[t, d - 1].astype(jnp.float32)
        outs[a][:, pl.ds(p * width, width)] = total.astype(jnp.bfloat16)
    for t in range(len(tasks)):
        c_copy(t).wait_send()
        y_copy(t).wait_send()
        for d in range(1, nz):
            z_copy(t, d).wait_send()


def scatter_sum(n, part0, part1):
    nz = n // 4
    rows, width = part0.shape[0] // n, part0.shape[1]
    parts = 2
    tasks = 2 * parts
    wide = width // parts
    part0 = part0.reshape(nz, 2, 2, rows, width)
    part1 = part1.reshape(nz, 2, 2, rows, width)
    vmem = pl.BlockSpec(memory_space=pltpu.VMEM)
    out = jax.ShapeDtypeStruct((rows, width), jnp.bfloat16)
    dma = pltpu.SemaphoreType.DMA
    return pl.pallas_call(
        functools.partial(scatter_kernel, n, parts),
        in_specs=[vmem, vmem],
        out_specs=[vmem, vmem],
        out_shape=[out, out],
        scratch_shapes=[
            pltpu.VMEM((tasks, nz, 2, rows, wide), jnp.bfloat16),
            pltpu.VMEM((tasks, nz, 2, rows, wide), jnp.bfloat16),
            pltpu.VMEM((tasks, nz, rows, wide), jnp.bfloat16),
            pltpu.VMEM((tasks, nz, rows, wide), jnp.bfloat16),
            pltpu.VMEM((tasks, nz - 1, rows, wide), jnp.bfloat16),
            dma((tasks,)), dma((tasks,)), dma((tasks,)), dma((tasks,)), dma((tasks, nz - 1)), dma((tasks, nz - 1)),
        ],
        compiler_params=pltpu.CompilerParams(
            collective_id=1, has_side_effects=True, vmem_limit_bytes=40 * 1024 * 1024),
    )(part0, part1)


def dot(a, b, da, db):
    return lax.dot_general(a, b, (((da,), (db,)), ((), ())), preferred_element_type=jnp.float32)


def per_device(n, tokens, grad_out, gate_base, up_base, down_base, gate_delta, up_delta, down_delta, offsets, seeds):
    gate_w, up_w, down_w, tok_all, grad_all = merge_and_gather(
        n, offsets[:, 0], seeds, tokens, grad_out, gate_base.T, up_base.T, down_base,
        jnp.swapaxes(gate_delta, 1, 2), jnp.swapaxes(up_delta, 1, 2), down_delta)
    total = n * tokens.shape[0]
    tok_all = tok_all.reshape(total, tokens.shape[1])
    grad_all = grad_all.reshape(total, tokens.shape[1])
    gate_pre = dot(gate_w, tok_all, 1, 1)
    up_pre = dot(up_w, tok_all, 1, 1)
    sigmoid_gate = jax.nn.sigmoid(gate_pre)
    hidden = (gate_pre * sigmoid_gate * up_pre).astype(jnp.bfloat16)
    grad_hidden = dot(down_w, grad_all, 1, 1)
    grad_gate_act = (
        grad_hidden * up_pre * sigmoid_gate * (1.0 + gate_pre * (1.0 - sigmoid_gate))
    ).astype(jnp.bfloat16)
    grad_up_act = (grad_hidden * gate_pre * sigmoid_gate).astype(jnp.bfloat16)
    mixed_part = dot(hidden, down_w, 0, 0).astype(jnp.bfloat16)
    grad_tok_part = (dot(grad_gate_act, gate_w, 0, 0) + dot(grad_up_act, up_w, 0, 0)).astype(jnp.bfloat16)
    mixed, grad_tokens = scatter_sum(n, mixed_part, grad_tok_part)
    grad_down = dot(hidden, grad_all, 1, 0).astype(jnp.bfloat16)
    grad_gate = dot(grad_gate_act, tok_all, 1, 0).astype(jnp.bfloat16)
    grad_up = dot(grad_up_act, tok_all, 1, 0).astype(jnp.bfloat16)
    return mixed, grad_tokens, grad_gate.T, grad_up.T, grad_down


def solution(mesh):
    both = P(("groups", "tensor"), None)
    return jax.shard_map(
        functools.partial(per_device, mesh.shape["tensor"]),
        mesh=mesh,
        in_specs=(
            both, both, P(None, "tensor"), P(None, "tensor"), P("tensor", None),
            P(None, None, "tensor"), P(None, None, "tensor"), P(None, "tensor", None),
            P(None, "tensor"), P("groups"),
        ),
        out_specs=(both, both, P("groups", "tensor"), P("groups", "tensor"), both),
        check_vma=False,
    )
```

time: 283 us -> 139 us (0.49)
  waiting for transfers between devices: 150 us -> 0 us
  Pallas kernels: 0 us -> 102 us
  other arithmetic: 65.9 us -> 0 us
  between operations: 15.2 us -> 0.72 us
  matrix products: 43 us -> 31.2 us
  local copies, waits for them, and re-layouts: 7.71 us -> 4.47 us
    reduce_scatter x2 -> x0, waiting for transfers between devices: 135 us -> none  [the longest x1 79.5 us: per_device(): lax.psum_scatter(jnp.dot(rows_block, down_w, preferred_element_type=jnp.f...]
    pallas_call x0 -> x2, Pallas kernels: none -> 102 us  [the longest x1 55.7 us: merge_and_gather(): pl.pallas_call(functools.partial(merge_kernel, n), grid=(width // COLS,),...]
    convert_element_type x4 -> x0, other arithmetic: 64 us -> none  [the longest x2 60.7 us: merge_shard(): (base.astype(jnp.float32) + 5.0 * (first + second)).astype(jnp.bfloat16)]
    all_gather x2 -> x0, waiting for transfers between devices: 14.1 us -> none  [the longest x1 14.1 us: per_device(): grad_all = lax.all_gather(grad_out, 'tensor', axis=0, tiled=True)]
    dot_general x6 -> x9, matrix products: 43 us -> 31.2 us  [dot(): lax.dot_general(a, b, (((da,), (db,)), ((), ())), preferred_element_type=...]
    slice x3 -> x0, local copies, waits for them, and re-layouts: 6.46 us -> none  [the longest x1 3.79 us: per_device(): grad_pair[:, slab_cols:]]
    unnamed x24 -> x12, local copies, waits for them, and re-layouts: 1.26 us -> 4.47 us
  transfers between devices with their start and end apart: 4 -> 0, of which waited for: 3 -> 0; matrix products, arithmetic and copies ran while one was open for 35% -> 0% of each run, Pallas kernels for 0% -> 0%
where the time goes in v1:
time: 139 us; the launch traced here: 138 us
  Pallas kernels  102 us (73%)
  matrix products  31.2 us (22%)
  local copies, waits for them, and re-layouts  4.47 us (3%)
    pallas_call x1, Pallas kernels, merge_and_gather(): pl.pallas_call(functools.partial(merge_kernel, n), grid=(width // COLS,),...  55.7 us
    pallas_call x1, Pallas kernels, scatter_sum(): pl.pallas_call(functools.partial(scatter_kernel, n, parts), in_specs=[vme...  46.4 us
    dot_general x9, matrix products, dot(): lax.dot_general(a, b, (((da,), (db,)), ((), ())), preferred_element_type=...  31.2 us
    unnamed x12, local copies, waits for them, and re-layouts  4.47 us

profile of v1, /device:TPU:0, one launch (start us, length us, event | category | flops | bytes accessed | tf_op | source)
XLA Modules:
  0.0 138.4 jit_solution(6710316349585792819)
XLA Ops:
  0.6 0.0 copy-start
  0.6 0.9 copy-done
  1.6 0.0 copy-start.1
  1.6 0.9 copy-done.1
  2.5 0.0 copy-start.2
  2.5 0.7 copy-done.2
  3.1 0.0 copy-start.3
  3.1 0.7 copy-done.3
  3.8 55.7 %shard_map.137 = (bf16[864,2560]{1,0:T(8,128)(2,1)S(1)}, bf16[864,2560]{1,0:T(8,128)(2,1)S(1)}, bf16[864,2560]{1,0:T(8,128)(2,1)}, bf16[4,2,2,32,2560]{4,3,2,1,0...) custom-call(s32[3]{0:T(128)S(1)} %bitcast.29, s32[2]{0:T(128)S(1)} %copy-done.3, bf16[32,2560]{1,0:T(8,128)(2,1)S(1)} %copy-done, ...), custom_call_target="tpu_custom_call" | custom-call | tf_op jit(solution)/shard_map/pallas_call | solution.py:184
  59.4 2.5 %fusion.1 = f32[864,512]{1,0:T(8,128)S(1)} fusion(bf16[864,2560]{1,0:T(8,128)(2,1)S(1)} %get-tuple-element.14, bf16[512,2560]{1,0:T(8,128)(2,1)S(1)} %bitcast.30), kind=kOutput, calls=%fused_computation.10 | convolution fusion | flops 2264924160 | bytes 8814592 | tf_op jit(solution)/shard_map/dot_general | solution.py:302
  61.9 0.0 copy-start.4
  61.9 2.5 %fusion = f32[864,512]{1,0:T(8,128)S(1)} fusion(bf16[864,2560]{1,0:T(8,128)(2,1)S(1)} %get-tuple-element.12, bf16[512,2560]{1,0:T(8,128)(2,1)S(1)} %bitcast.31), kind=kOutput, calls=%fused_computation.9 | convolution fusion | flops 2264924160 | bytes 8814592 | tf_op jit(solution)/shard_map/dot_general | solution.py:302
  64.4 0.0 copy-done.4
  64.4 3.2 %multiply_convert_fusion = (bf16[864,512]{1,0:T(8,128)(2,1)S(1)}, bf16[864,512]{1,0:T(8,128)(2,1)S(1)}, bf16[864,512]{1,0:T(8,128)(2,1)S(1)}) fusion(f32[864,512]{1,0:T(8,128)S(1)} %fusion, f32[864,512]{1,0:T(8,128)S(1)} %fusion.1, bf16[864,2560]{1,0:T(8,128)(2,1)S(1)} %copy-done.4, bf16[512,2560]{1,0:T(8,128)(2,1)S(1)} %bitcast.34), kind=kOutput, calls=%fused_computation.5 | convolution fusion | flops 2272002048 | bytes 13238272 | tf_op jit(solution)/shard_map/dot_general | solution.py:302
  67.6 3.2 %convolution_convert_fusion.3 = bf16[512,2560]{1,0:T(8,128)(2,1)S(1)} fusion(bf16[864,512]{1,0:T(8,128)(2,1)S(1)} %get-tuple-element.21, bf16[864,2560]{1,0:T(8,128)(2,1)S(1)} %copy-done.4), kind=kOutput, calls=%fused_computation.4 | convolution fusion | flops 2266234880 | bytes 7929856 | tf_op jit(solution)/shard_map/dot_general | solution.py:302
  70.8 3.0 %fusion.2 = f32[512,2560]{1,0:T(8,128)S(1)} fusion(bf16[864,512]{1,0:T(8,128)(2,1)S(1)} %get-tuple-element.20, bf16[864,2560]{1,0:T(8,128)(2,1)S(1)} %get-tuple-element.12), kind=kOutput, calls=%fused_computation.11 | convolution fusion | flops 2264924160 | bytes 10551296 | tf_op jit(solution)/shard_map/dot_general | solution.py:302
  73.8 3.3 %add_convert_fusion = bf16[512,2560]{1,0:T(8,128)(2,1)S(1)} fusion(f32[512,2560]{1,0:T(8,128)S(1)} %fusion.2, bf16[864,512]{1,0:T(8,128)(2,1)S(1)} %get-tuple-element.19, bf16[864,2560]{1,0:T(8,128)(2,1)S(1)} %get-tuple-element.14), kind=kOutput, calls=%fused_computation.3 | convolution fusion | flops 2267545600 | bytes 13172736 | tf_op jit(solution)/shard_map/dot_general | solution.py:302
  77.0 46.4 %shard_map.138 = (bf16[32,2560]{1,0:T(8,128)(2,1)S(1)}, bf16[32,2560]{1,0:T(8,128)(2,1)S(1)}) custom-call(bf16[4,2,2,32,2560]{4,3,2,1,0:T(8,128)(2,1)S(1)} %bitcast.28, bf16[4,2,2,32,2560]{4,3,2,1,0:T(8,128)(2,1)S(1)} %bitcast.27), custom_call_target="tpu_custom_call" | custom-call | tf_op jit(solution)/shard_map/pallas_call | solution.py:283
  123.4 4.5 %convolution_convert_fusion.2 = bf16[864,2560]{1,0:T(8,128)(2,1)} fusion(bf16[864,512]{1,0:T(8,128)(2,1)S(1)} %get-tuple-element.21, bf16[512,2560]{1,0:T(8,128)(2,1)S(1)} %bitcast.35), kind=kOutput, calls=%fused_computation.2 | convolution fusion | flops 2267136000 | bytes 7929856 | tf_op jit(solution)/shard_map/dot_general | solution.py:302
  128.0 4.5 %convolution_convert_fusion = bf16[2560,864]{0,1:T(8,128)(2,1)} fusion(bf16[864,512]{1,0:T(8,128)(2,1)S(1)} %get-tuple-element.19, bf16[512,2560]{1,0:T(8,128)(2,1)S(1)} %bitcast.32), kind=kOutput, calls=%fused_computation | convolution fusion | flops 2267136000 | bytes 7929856 | tf_op jit(solution)/shard_map/dot_general | solution.py:302
  132.5 4.5 %convolution_convert_fusion.1 = bf16[2560,864]{0,1:T(8,128)(2,1)} fusion(bf16[864,512]{1,0:T(8,128)(2,1)S(1)} %get-tuple-element.20, bf16[512,2560]{1,0:T(8,128)(2,1)S(1)} %bitcast.33), kind=kOutput, calls=%fused_computation.1 | convolution fusion | flops 2267136000 | bytes 7929856 | tf_op jit(solution)/shard_map/dot_general | solution.py:302
  137.0 0.7 copy.17
  137.7 0.7 copy.18
Async XLA Ops:
  0.6 0.9 copy-start
  1.6 0.9 copy-start.1
  2.5 0.7 copy-start.2
  3.1 0.7 copy-start.3
  61.9 2.5 %copy-start.4 = (bf16[864,2560]{1,0:T(8,128)(2,1)S(1)}, bf16[864,2560]{1,0:T(8,128)(2,1)}, u32[]{:S(2)}) copy-start(bf16[864,2560]{1,0:T(8,128)(2,1)} %get-tuple-element.15) | copy-start | bytes 13271044

commit v2 on v1

--- a/solution.py
+++ b/solution.py
@@ -196,17 +196,35 @@
     )(offs, seeds, tok, grd, gb, ub, db, gd, ud, dd)
 
 
-def scatter_kernel(
-    n, parts, part0, part1, out0, out1,
-    got_c, sum_c, got_y, sum_y, got_z, cs, cr, ys, yr, zs, zr,
+def dot(a, b, da, db):
+    return lax.dot_general(a, b, (((da,), (db,)), ((), ())), preferred_element_type=jnp.float32)
+
+
+TILE = 256
+
+
+def finish_kernel(
+    n, parts, hid_in, ga_in, ua_in, gw_in, uw_in, dw_in, tok_in, grd_in,
+    out0, out1, grad_gate, grad_up, grad_down,
+    hid, ga, ua, gw, uw, dw, tok, grd, part0, part1, stage,
+    got_c, sum_c, got_y, sum_y, got_z, load_sem, stage_sem, cs, cr, ys, yr, zs, zr,
 ):
     nz = n // 4
     z, y, c = place(n)
     width = out0.shape[1] // parts
+    rows = out0.shape[0]
     parts_in, outs = (part0, part1), (out0, out1)
 
     def index(zz, yy, cc):
         return {"tensor": (zz * 2 + yy) * 2 + cc}
+
+    loads = [
+        pltpu.make_async_copy(src, dst, load_sem.at[i])
+        for i, (src, dst) in enumerate((
+            (hid_in, hid), (dw_in, dw), (ga_in, ga), (ua_in, ua), (gw_in, gw), (uw_in, uw), (grd_in, grd), (tok_in, tok)))
+    ]
+    for load in loads:
+        load.start()
 
     barrier = pltpu.get_barrier_semaphore()
     for d in range(1, nz):
@@ -234,9 +252,8 @@
             src_ref=sum_y.at[t, zz], dst_ref=got_z.at[t, d - 1],
             send_sem=zs.at[t, d - 1], recv_sem=zr.at[t, d - 1], device_id=index(zz, y, c), device_id_type=MESH)
 
-    for t in range(len(tasks)):
-        c_copy(t).start()
-    for t, (a, p) in enumerate(tasks):
+    def core_step(t):
+        a, p = tasks[t]
         c_copy(t).wait_recv()
 
         @pl.loop(0, nz)
@@ -246,7 +263,8 @@
                 sum_c[t, zz, yy] = (mine + got_c[t, zz, yy].astype(jnp.float32)).astype(jnp.bfloat16)
 
         y_copy(t).start()
-    for t in range(len(tasks)):
+
+    def y_step(t):
         y_copy(t).wait_recv()
 
         @pl.loop(0, nz)
@@ -256,12 +274,68 @@
 
         for d in range(1, nz):
             z_copy(t, d).start()
-    for t, (a, p) in enumerate(tasks):
+
+    def z_step(t):
+        a, p = tasks[t]
         total = sum_y[t, z].astype(jnp.float32)
         for d in range(1, nz):
             z_copy(t, d).wait_recv()
             total = total + got_z[t, d - 1].astype(jnp.float32)
         outs[a][:, pl.ds(p * width, width)] = total.astype(jnp.bfloat16)
+
+    def partial_sums(t, pairs):
+        a, p = tasks[t]
+
+        @pl.loop(0, width // TILE)
+        def _(i):
+            cols = pl.ds(pl.multiple_of(p * width + i * TILE, TILE), TILE)
+            total = dot(pairs[0][0][...], pairs[0][1][:, cols], 0, 0)
+            for left, right in pairs[1:]:
+                total = total + dot(left[...], right[:, cols], 0, 0)
+            parts_in[a][:, :, :, :, cols] = total.reshape(nz, 2, 2, rows, TILE).astype(jnp.bfloat16)
+
+        c_copy(t).start()
+
+    def weight_grad(left, right, out, used):
+        @pl.loop(0, out.shape[1] // (2 * TILE))
+        def _(i):
+            for slot in range(2):
+                cols = pl.ds(pl.multiple_of((2 * i + slot) * TILE, TILE), TILE)
+                copy = pltpu.make_async_copy(stage.at[slot], out.at[:, cols], stage_sem.at[slot])
+                if used:
+                    copy.wait()
+                else:
+                    @pl.when(i > 0)
+                    def _():
+                        copy.wait()
+                stage[slot] = dot(left[...], right[:, cols], 1, 0).astype(jnp.bfloat16)
+                copy.start()
+
+    loads[0].wait()
+    loads[1].wait()
+    partial_sums(0, [(hid, dw)])
+    partial_sums(1, [(hid, dw)])
+    core_step(0)
+    for load in loads[2:6]:
+        load.wait()
+    partial_sums(2, [(ga, gw), (ua, uw)])
+    core_step(1)
+    partial_sums(3, [(ga, gw), (ua, uw)])
+    core_step(2)
+    loads[6].wait()
+    loads[7].wait()
+    y_step(0)
+    core_step(3)
+    weight_grad(hid, grd, grad_down, False)
+    y_step(1)
+    weight_grad(ga, tok, grad_gate, True)
+    y_step(2)
+    weight_grad(ua, tok, grad_up, True)
+    y_step(3)
+    for slot in range(2):
+        pltpu.make_async_copy(stage.at[slot], grad_up.at[:, pl.ds(0, TILE)], stage_sem.at[slot]).wait()
+    for t in range(len(tasks)):
+        z_step(t)
     for t in range(len(tasks)):
         c_copy(t).wait_send()
         y_copy(t).wait_send()
@@ -269,37 +343,39 @@
             z_copy(t, d).wait_send()
 
 
-def scatter_sum(n, part0, part1):
+def finish(n, hid, ga, ua, gw, uw, dw, tok, grd):
     nz = n // 4
-    rows, width = part0.shape[0] // n, part0.shape[1]
+    total, width = tok.shape
+    rows = total // n
     parts = 2
     tasks = 2 * parts
     wide = width // parts
-    part0 = part0.reshape(nz, 2, 2, rows, width)
-    part1 = part1.reshape(nz, 2, 2, rows, width)
     vmem = pl.BlockSpec(memory_space=pltpu.VMEM)
+    anyspace = pl.BlockSpec(memory_space=pl.ANY)
     out = jax.ShapeDtypeStruct((rows, width), jnp.bfloat16)
+    grad = jax.ShapeDtypeStruct(gw.shape, jnp.bfloat16)
     dma = pltpu.SemaphoreType.DMA
+    arrays = (hid, ga, ua, gw, uw, dw, tok, grd)
     return pl.pallas_call(
-        functools.partial(scatter_kernel, n, parts),
-        in_specs=[vmem, vmem],
-        out_specs=[vmem, vmem],
-        out_shape=[out, out],
-        scratch_shapes=[
+        functools.partial(finish_kernel, n, parts),
+        in_specs=[anyspace] * 8,
+        out_specs=[vmem, vmem, anyspace, anyspace, anyspace],
+        out_shape=[out, out, grad, grad, grad],
+        scratch_shapes=[pltpu.VMEM(x.shape, x.dtype) for x in arrays] + [
+            pltpu.VMEM((nz, 2, 2, rows, width), jnp.bfloat16),
+            pltpu.VMEM((nz, 2, 2, rows, width), jnp.bfloat16),
+            pltpu.VMEM((2, gw.shape[0], TILE), jnp.bfloat16),
             pltpu.VMEM((tasks, nz, 2, rows, wide), jnp.bfloat16),
             pltpu.VMEM((tasks, nz, 2, rows, wide), jnp.bfloat16),
             pltpu.VMEM((tasks, nz, rows, wide), jnp.bfloat16),
             pltpu.VMEM((tasks, nz, rows, wide), jnp.bfloat16),
             pltpu.VMEM((tasks, nz - 1, rows, wide), jnp.bfloat16),
+            dma((8,)), dma((2,)),
             dma((tasks,)), dma((tasks,)), dma((tasks,)), dma((tasks,)), dma((tasks, nz - 1)), dma((tasks, nz - 1)),
         ],
         compiler_params=pltpu.CompilerParams(
-            collective_id=1, has_side_effects=True, vmem_limit_bytes=40 * 1024 * 1024),
-    )(part0, part1)
-
-
-def dot(a, b, da, db):
-    return lax.dot_general(a, b, (((da,), (db,)), ((), ())), preferred_element_type=jnp.float32)
+            collective_id=1, has_side_effects=True, vmem_limit_bytes=48 * 1024 * 1024),
+    )(*arrays)
 
 
 def per_device(n, tokens, grad_out, gate_base, up_base, down_base, gate_delta, up_delta, down_delta, offsets, seeds):
@@ -318,12 +394,8 @@
         grad_hidden * up_pre * sigmoid_gate * (1.0 + gate_pre * (1.0 - sigmoid_gate))
     ).astype(jnp.bfloat16)
     grad_up_act = (grad_hidden * gate_pre * sigmoid_gate).astype(jnp.bfloat16)
-    mixed_part = dot(hidden, down_w, 0, 0).astype(jnp.bfloat16)
-    grad_tok_part = (dot(grad_gate_act, gate_w, 0, 0) + dot(grad_up_act, up_w, 0, 0)).astype(jnp.bfloat16)
-    mixed, grad_tokens = scatter_sum(n, mixed_part, grad_tok_part)
-    grad_down = dot(hidden, grad_all, 1, 0).astype(jnp.bfloat16)
-    grad_gate = dot(grad_gate_act, tok_all, 1, 0).astype(jnp.bfloat16)
-    grad_up = dot(grad_up_act, tok_all, 1, 0).astype(jnp.bfloat16)
+    mixed, grad_tokens, grad_gate, grad_up, grad_down = finish(
+        n, hidden, grad_gate_act, grad_up_act, gate_w, up_w, down_w, tok_all, grad_all)
     return mixed, grad_tokens, grad_gate.T, grad_up.T, grad_down
 
 

time: 139 us -> 133 us (0.957)
  matrix products: 31.2 us -> 8.11 us
  local copies, waits for them, and re-layouts: 4.47 us -> 16.2 us
  Pallas kernels: 102 us -> 107 us
    dot_general x9 -> x3, matrix products: 31.2 us -> 8.11 us  [dot(): lax.dot_general(a, b, (((da,), (db,)), ((), ())), preferred_element_type=...]
    unnamed x12 -> x31, local copies, waits for them, and re-layouts: 4.47 us -> 16.2 us
    pallas_call x1, Pallas kernels: 46.4 us -> 51.7 us  [finish(): pl.pallas_call(functools.partial(finish_kernel, n, parts), in_specs=[anys...]
where the time goes in v2:
time: 133 us; the launch traced here: 132 us
  Pallas kernels  107 us (80%)
  local copies, waits for them, and re-layouts  16.2 us (12%)
  matrix products  8.11 us (6%)
    pallas_call x1, Pallas kernels, merge_and_gather(): pl.pallas_call(functools.partial(merge_kernel, n), grid=(width // COLS,),...  55.7 us
    pallas_call x1, Pallas kernels, finish(): pl.pallas_call(functools.partial(finish_kernel, n, parts), in_specs=[anys...  51.7 us
    unnamed x31, local copies, waits for them, and re-layouts  16.2 us
    dot_general x3, matrix products, dot(): lax.dot_general(a, b, (((da,), (db,)), ((), ())), preferred_element_type=...  8.11 us

profile of v2, /device:TPU:0, one launch (start us, length us, event | category | flops | bytes accessed | tf_op | source)
XLA Modules:
  0.0 132.4 jit_solution(18304109443536221118)
XLA Ops:
  0.6 0.0 copy-start.5
  0.6 0.9 copy-done.5
  1.6 0.0 copy-start.6
  1.6 0.9 copy-done.6
  2.5 0.0 copy-start.7
  2.5 0.7 copy-done.7
  3.1 0.0 copy-start.8
  3.1 0.7 copy-done.8
  3.8 55.7 %shard_map.137 = (bf16[864,2560]{1,0:T(8,128)(2,1)S(1)}, bf16[864,2560]{1,0:T(8,128)(2,1)S(1)}, bf16[864,2560]{1,0:T(8,128)(2,1)}, bf16[4,2,2,32,2560]{4,3,2,1,0...) custom-call(s32[3]{0:T(128)S(1)} %bitcast.20, s32[2]{0:T(128)S(1)} %copy-done.8, bf16[32,2560]{1,0:T(8,128)(2,1)S(1)} %copy-done.5, ...), custom_call_target="tpu_custom_call" | custom-call | tf_op jit(solution)/shard_map/pallas_call | solution.py:184
  59.4 0.0 copy-start
  59.5 0.0 copy-start.1
  59.5 0.0 copy-start.2
  59.5 0.0 copy-start.4
  59.5 2.5 %fusion.1 = f32[864,512]{1,0:T(8,128)S(1)} fusion(bf16[864,2560]{1,0:T(8,128)(2,1)S(1)} %get-tuple-element.17.uw_in, bf16[512,2560]{1,0:T(8,128)(2,1)S(1)} %bitcast.15), kind=kOutput, calls=%fused_computation.5 | convolution fusion | flops 2264924160 | bytes 8814592 | tf_op jit(solution)/shard_map/dot_general | solution.py:200
  62.0 0.0 copy-done
  62.0 1.0 copy-done.1
  63.0 0.7 copy-done.2
  63.7 0.0 copy-start.9
  63.7 2.5 %fusion = f32[864,512]{1,0:T(8,128)S(1)} fusion(bf16[864,2560]{1,0:T(8,128)(2,1)S(1)} %get-tuple-element.15.gw_in, bf16[512,2560]{1,0:T(8,128)(2,1)S(1)} %bitcast.16), kind=kOutput, calls=%fused_computation.4 | convolution fusion | flops 2264924160 | bytes 8814592 | tf_op jit(solution)/shard_map/dot_general | solution.py:200
  66.2 0.0 copy-done.4
  66.2 0.0 copy-done.9
  66.2 0.0 copy-start.3
  66.2 3.2 %multiply_convert_fusion = (bf16[864,512]{1,0:T(8,128)(2,1)S(1)}, bf16[864,512]{1,0:T(8,128)(2,1)S(1)}, bf16[864,512]{1,0:T(8,128)(2,1)S(1)}) fusion(f32[864,512]{1,0:T(8,128)S(1)} %fusion, f32[864,512]{1,0:T(8,128)S(1)} %fusion.1, bf16[864,2560]{1,0:T(8,128)(2,1)S(1)} %copy-done.9, bf16[512,2560]{1,0:T(8,128)(2,1)S(1)} %bitcast.18), kind=kOutput, calls=%fused_computation | convolution fusion | flops 2272002048 | bytes 13238272 | tf_op jit(solution)/shard_map/dot_general | solution.py:200
  69.4 0.0 copy-done.3
  69.4 51.7 %shard_map.138 = (bf16[32,2560]{1,0:T(8,128)(2,1)S(1)}, bf16[32,2560]{1,0:T(8,128)(2,1)S(1)}, bf16[864,2560]{1,0:T(8,128)(2,1)}, bf16[864,2560]{1,0:T(8,128)(2,1)}, bf16[864,2560]{1,0:T(8,128)(2,1)}) custom-call(bf16[864,512]{1,0:T(8,128)(2,1)S(1)} %get-tuple-element.27.hid_in, bf16[864,512]{1,0:T(8,128)(2,1)S(1)} %get-tuple-element.26.ga_in, ...), custom_call_target="tpu_custom_call" | custom-call | tf_op jit(solution)/shard_map/pallas_call | solution.py:359
  121.1 0.7 copy.20
  121.8 0.7 copy.21
  122.4 0.0 copy-start.10
  122.4 0.0 slice-start
  122.4 4.9 %copy.22 = bf16[2560,864]{0,1:T(8,128)(2,1)} copy(bf16[2560,864]{0,1:T(8,128)(2,1)} %bitcast.26) | data formatting | bytes 8847360
  127.4 0.0 copy-done.10
  127.4 0.0 slice-start.1
  127.4 2.1 %copy.23 = bf16[2560,864]{0,1:T(8,128)(2,1)} copy(bf16[2560,864]{0,1:T(8,128)(2,1)S(1)} %bitcast.25) | data formatting | bytes 8847360
  129.5 0.6 slice-done
  130.1 0.2 slice-done.1
  130.3 2.1 %copy.24 = bf16[864,2560]{1,0:T(8,128)(2,1)} copy(bf16[864,2560]{1,0:T(8,128)(2,1)S(1)} %bitcast.24) | data formatting | bytes 8847360
  (1 shorter events, 0.0 us)
Async XLA Ops:
  0.6 0.9 copy-start.5
  1.6 0.9 copy-start.6
  2.5 0.7 copy-start.7
  3.1 0.7 copy-start.8
  59.4 2.5 %copy-start = (bf16[864,2560]{1,0:T(8,128)(2,1)}, bf16[864,2560]{1,0:T(8,128)(2,1)S(1)}, u32[]{:S(2)}) copy-start(bf16[864,2560]{1,0:T(8,128)(2,1)S(1)} %get-tuple-element.15.gw_in) | copy-start | bytes 13271044
  59.5 3.5 %copy-start.1 = (bf16[864,2560]{1,0:T(8,128)(2,1)}, bf16[864,2560]{1,0:T(8,128)(2,1)S(1)}, u32[]{:S(2)}) copy-start(bf16[864,2560]{1,0:T(8,128)(2,1)S(1)} %get-tuple-element.17.uw_in) | copy-start | bytes 13271044
  59.5 4.3 %copy-start.2 = (bf16[4,2,2,32,2560]{4,3,2,1,0:T(8,128)(2,1)}, bf16[4,2,2,32,2560]{4,3,2,1,0:T(8,128)(2,1)S(1)}, u32[]{:S(2)}) copy-start(bf16[4,2,2,32,2560]{4,3,2,1,0:T(8,128)(2,1)S(1)} %get-tuple-element.16) | copy-start | bytes 7864324
  59.5 6.7 %copy-start.4 = (bf16[4,2,2,32,2560]{4,3,2,1,0:T(8,128)(2,1)}, bf16[4,2,2,32,2560]{4,3,2,1,0:T(8,128)(2,1)S(1)}, u32[]{:S(2)}) copy-start(bf16[4,2,2,32,2560]{4,3,2,1,0:T(8,128)(2,1)S(1)} %get-tuple-element.19) | copy-start | bytes 7864324
  63.7 2.5 %copy-start.9 = (bf16[864,2560]{1,0:T(8,128)(2,1)S(1)}, bf16[864,2560]{1,0:T(8,128)(2,1)}, u32[]{:S(2)}) copy-start(bf16[864,2560]{1,0:T(8,128)(2,1)} %get-tuple-element.18.dw_in) | copy-start | bytes 13271044
  66.2 3.2 %copy-start.3 = (bf16[4,2,2,32,2560]{4,3,2,1,0:T(8,128)(2,1)S(1)}, bf16[4,2,2,32,2560]{4,3,2,1,0:T(8,128)(2,1)}, u32[]{:S(2)}) copy-start(bf16[4,2,2,32,2560]{4,3,2,1,0:T(8,128)(2,1)} %copy-done.2) | copy-start | bytes 7864324
  122.4 5.0 %copy-start.10 = (bf16[864,2560]{1,0:T(8,128)(2,1)S(1)}, bf16[864,2560]{1,0:T(8,128)(2,1)}, u32[]{:S(2)}) copy-start(bf16[864,2560]{1,0:T(8,128)(2,1)} %get-tuple-element.23) | copy-start | bytes 13271044
  122.4 7.7 %slice-start = ((s8[4423680]{0:T(1024)(128)(4,1)}), s8[4194304]{0:T(1024)(128)(4,1)S(1)}, s32[]{:S(2)}) async-start(s8[4423680]{0:T(1024)(128)(4,1)} %bitcast.23), calls=%async_computation | async-start | bytes 8388608
  127.4 3.0 %slice-start.1 = ((s8[4423680]{0:T(1024)(128)(4,1)}), s8[229376]{0:T(1024)(128)(4,1)S(1)}, s32[]{:S(2)}) async-start(s8[4423680]{0:T(1024)(128)(4,1)} %bitcast.23), calls=%async_computation.1 | async-start | bytes 458752

commit v3 on v2

--- a/solution.py
+++ b/solution.py
@@ -140,13 +140,13 @@
     def _():
         forward_y(0)
 
-    @pl.when(step == last * 14 // 19)
+    @pl.when(step == last * 13 // 19)
+    def _():
+        forward_y(1)
+
+    @pl.when(step == last * 16 // 19)
     def _():
         forward_c(0)
-
-    @pl.when(step == last * 16 // 19)
-    def _():
-        forward_y(1)
 
     shard = gb.shape[0]
     seed0 = seeds[0] * jnp.int32(MUL_S)
@@ -206,7 +206,7 @@
 def finish_kernel(
     n, parts, hid_in, ga_in, ua_in, gw_in, uw_in, dw_in, tok_in, grd_in,
     out0, out1, grad_gate, grad_up, grad_down,
-    hid, ga, ua, gw, uw, dw, tok, grd, part0, part1, stage,
+    hid, ga, ua, gw, uw, dw, tok, grd, hid_t, ga_t, ua_t, part0, part1, stage,
     got_c, sum_c, got_y, sum_y, got_z, load_sem, stage_sem, cs, cr, ys, yr, zs, zr,
 ):
     nz = n // 4
@@ -289,9 +289,9 @@
         @pl.loop(0, width // TILE)
         def _(i):
             cols = pl.ds(pl.multiple_of(p * width + i * TILE, TILE), TILE)
-            total = dot(pairs[0][0][...], pairs[0][1][:, cols], 0, 0)
+            total = dot(pairs[0][0][...], pairs[0][1][:, cols], 1, 0)
             for left, right in pairs[1:]:
-                total = total + dot(left[...], right[:, cols], 0, 0)
+                total = total + dot(left[...], right[:, cols], 1, 0)
             parts_in[a][:, :, :, :, cols] = total.reshape(nz, 2, 2, rows, TILE).astype(jnp.bfloat16)
 
         c_copy(t).start()
@@ -313,14 +313,17 @@
 
     loads[0].wait()
     loads[1].wait()
-    partial_sums(0, [(hid, dw)])
-    partial_sums(1, [(hid, dw)])
+    hid_t[...] = hid[...].T
+    partial_sums(0, [(hid_t, dw)])
+    partial_sums(1, [(hid_t, dw)])
     core_step(0)
     for load in loads[2:6]:
         load.wait()
-    partial_sums(2, [(ga, gw), (ua, uw)])
+    ga_t[...] = ga[...].T
+    ua_t[...] = ua[...].T
+    partial_sums(2, [(ga_t, gw), (ua_t, uw)])
     core_step(1)
-    partial_sums(3, [(ga, gw), (ua, uw)])
+    partial_sums(3, [(ga_t, gw), (ua_t, uw)])
     core_step(2)
     loads[6].wait()
     loads[7].wait()
@@ -362,6 +365,9 @@
         out_specs=[vmem, vmem, anyspace, anyspace, anyspace],
         out_shape=[out, out, grad, grad, grad],
         scratch_shapes=[pltpu.VMEM(x.shape, x.dtype) for x in arrays] + [
+            pltpu.VMEM(hid.shape[::-1], hid.dtype),
+            pltpu.VMEM(hid.shape[::-1], hid.dtype),
+            pltpu.VMEM(hid.shape[::-1], hid.dtype),
             pltpu.VMEM((nz, 2, 2, rows, width), jnp.bfloat16),
             pltpu.VMEM((nz, 2, 2, rows, width), jnp.bfloat16),
             pltpu.VMEM((2, gw.shape[0], TILE), jnp.bfloat16),

time: 133 us -> 130 us (0.977)
  Pallas kernels: 107 us -> 105 us
    pallas_call x1, Pallas kernels: 55.7 us -> 51.1 us  [merge_and_gather(): pl.pallas_call(functools.partial(merge_kernel, n), grid=(width // COLS,),...]
    pallas_call x1, Pallas kernels: 51.7 us -> 53.9 us  [finish(): pl.pallas_call(functools.partial(finish_kernel, n, parts), in_specs=[anys...]
where the time goes in v3:
time: 130 us
  Pallas kernels  105 us (81%)
  local copies, waits for them, and re-layouts  16.2 us (12%)
  matrix products  8.11 us (6%)
    pallas_call x1, Pallas kernels, finish(): pl.pallas_call(functools.partial(finish_kernel, n, parts), in_specs=[anys...  53.9 us
    pallas_call x1, Pallas kernels, merge_and_gather(): pl.pallas_call(functools.partial(merge_kernel, n), grid=(width // COLS,),...  51.1 us
    unnamed x31, local copies, waits for them, and re-layouts  16.2 us
    dot_general x3, matrix products, dot(): lax.dot_general(a, b, (((da,), (db,)), ((), ())), preferred_element_type=...  8.11 us

profile of v3, /device:TPU:0, one launch (start us, length us, event | category | flops | bytes accessed | tf_op | source)
XLA Modules:
  0.0 130.1 jit_solution(1921507932218224878)
XLA Ops:
  0.6 0.0 copy-start.5
  0.6 0.9 copy-done.5
  1.6 0.0 copy-start.6
  1.6 0.9 copy-done.6
  2.5 0.0 copy-start.7
  2.5 0.7 copy-done.7
  3.1 0.0 copy-start.8
  3.1 0.7 copy-done.8
  3.8 51.1 %shard_map.137 = (bf16[864,2560]{1,0:T(8,128)(2,1)S(1)}, bf16[864,2560]{1,0:T(8,128)(2,1)S(1)}, bf16[864,2560]{1,0:T(8,128)(2,1)}, bf16[4,2,2,32,2560]{4,3,2,1,0...) custom-call(s32[3]{0:T(128)S(1)} %bitcast.20, s32[2]{0:T(128)S(1)} %copy-done.8, bf16[32,2560]{1,0:T(8,128)(2,1)S(1)} %copy-done.5, ...), custom_call_target="tpu_custom_call" | custom-call | tf_op jit(solution)/shard_map/pallas_call | solution.py:184
  54.9 0.0 copy-start
  54.9 0.0 copy-start.1
  54.9 0.0 copy-start.2
  55.0 0.0 copy-start.4
  55.0 2.5 %fusion.1 = f32[864,512]{1,0:T(8,128)S(1)} fusion(bf16[864,2560]{1,0:T(8,128)(2,1)S(1)} %get-tuple-element.17.uw_in, bf16[512,2560]{1,0:T(8,128)(2,1)S(1)} %bitcast.15), kind=kOutput, calls=%fused_computation.5 | convolution fusion | flops 2264924160 | bytes 8814592 | tf_op jit(solution)/shard_map/dot_general | solution.py:200
  57.4 0.0 copy-done
  57.5 1.0 copy-done.1
  58.5 0.7 copy-done.2
  59.2 0.0 copy-start.9
  59.2 2.5 %fusion = f32[864,512]{1,0:T(8,128)S(1)} fusion(bf16[864,2560]{1,0:T(8,128)(2,1)S(1)} %get-tuple-element.15.gw_in, bf16[512,2560]{1,0:T(8,128)(2,1)S(1)} %bitcast.16), kind=kOutput, calls=%fused_computation.4 | convolution fusion | flops 2264924160 | bytes 8814592 | tf_op jit(solution)/shard_map/dot_general | solution.py:200
  61.7 0.0 copy-done.4
  61.7 0.0 copy-done.9
  61.7 0.0 copy-start.3
  61.7 3.2 %multiply_convert_fusion = (bf16[864,512]{1,0:T(8,128)(2,1)S(1)}, bf16[864,512]{1,0:T(8,128)(2,1)S(1)}, bf16[864,512]{1,0:T(8,128)(2,1)S(1)}) fusion(f32[864,512]{1,0:T(8,128)S(1)} %fusion, f32[864,512]{1,0:T(8,128)S(1)} %fusion.1, bf16[864,2560]{1,0:T(8,128)(2,1)S(1)} %copy-done.9, bf16[512,2560]{1,0:T(8,128)(2,1)S(1)} %bitcast.18), kind=kOutput, calls=%fused_computation | convolution fusion | flops 2272002048 | bytes 13238272 | tf_op jit(solution)/shard_map/dot_general | solution.py:200
  64.9 0.0 copy-done.3
  64.9 53.9 %shard_map.138 = (bf16[32,2560]{1,0:T(8,128)(2,1)S(1)}, bf16[32,2560]{1,0:T(8,128)(2,1)S(1)}, bf16[864,2560]{1,0:T(8,128)(2,1)}, bf16[864,2560]{1,0:T(8,128)(2,1)}, bf16[864,2560]{1,0:T(8,128)(2,1)}) custom-call(bf16[864,512]{1,0:T(8,128)(2,1)S(1)} %get-tuple-element.27.hid_in, bf16[864,512]{1,0:T(8,128)(2,1)S(1)} %get-tuple-element.26.ga_in, ...), custom_call_target="tpu_custom_call" | custom-call | tf_op jit(solution)/shard_map/pallas_call | solution.py:362
  118.8 0.7 copy.20
  119.5 0.7 copy.21
  120.1 0.0 copy-start.10
  120.1 0.0 slice-start
  120.1 4.9 %copy.22 = bf16[2560,864]{0,1:T(8,128)(2,1)} copy(bf16[2560,864]{0,1:T(8,128)(2,1)} %bitcast.26) | data formatting | bytes 8847360
  125.1 0.0 copy-done.10
  125.1 0.0 slice-start.1
  125.1 2.1 %copy.23 = bf16[2560,864]{0,1:T(8,128)(2,1)} copy(bf16[2560,864]{0,1:T(8,128)(2,1)S(1)} %bitcast.25) | data formatting | bytes 8847360
  127.2 0.6 slice-done
  127.8 0.2 slice-done.1
  128.0 2.1 %copy.24 = bf16[864,2560]{1,0:T(8,128)(2,1)} copy(bf16[864,2560]{1,0:T(8,128)(2,1)S(1)} %bitcast.24) | data formatting | bytes 8847360
  (1 shorter events, 0.0 us)
Async XLA Ops:
  0.6 0.9 copy-start.5
  1.6 0.9 copy-start.6
  2.5 0.7 copy-start.7
  3.1 0.7 copy-start.8
  54.9 2.5 %copy-start = (bf16[864,2560]{1,0:T(8,128)(2,1)}, bf16[864,2560]{1,0:T(8,128)(2,1)S(1)}, u32[]{:S(2)}) copy-start(bf16[864,2560]{1,0:T(8,128)(2,1)S(1)} %get-tuple-element.15.gw_in) | copy-start | bytes 13271044
  54.9 3.5 %copy-start.1 = (bf16[864,2560]{1,0:T(8,128)(2,1)}, bf16[864,2560]{1,0:T(8,128)(2,1)S(1)}, u32[]{:S(2)}) copy-start(bf16[864,2560]{1,0:T(8,128)(2,1)S(1)} %get-tuple-element.17.uw_in) | copy-start | bytes 13271044
  54.9 4.3 %copy-start.2 = (bf16[4,2,2,32,2560]{4,3,2,1,0:T(8,128)(2,1)}, bf16[4,2,2,32,2560]{4,3,2,1,0:T(8,128)(2,1)S(1)}, u32[]{:S(2)}) copy-start(bf16[4,2,2,32,2560]{4,3,2,1,0:T(8,128)(2,1)S(1)} %get-tuple-element.16) | copy-start | bytes 7864324
  55.0 6.7 %copy-start.4 = (bf16[4,2,2,32,2560]{4,3,2,1,0:T(8,128)(2,1)}, bf16[4,2,2,32,2560]{4,3,2,1,0:T(8,128)(2,1)S(1)}, u32[]{:S(2)}) copy-start(bf16[4,2,2,32,2560]{4,3,2,1,0:T(8,128)(2,1)S(1)} %get-tuple-element.19) | copy-start | bytes 7864324
  59.2 2.5 %copy-start.9 = (bf16[864,2560]{1,0:T(8,128)(2,1)S(1)}, bf16[864,2560]{1,0:T(8,128)(2,1)}, u32[]{:S(2)}) copy-start(bf16[864,2560]{1,0:T(8,128)(2,1)} %get-tuple-element.18.dw_in) | copy-start | bytes 13271044
  61.7 3.2 %copy-start.3 = (bf16[4,2,2,32,2560]{4,3,2,1,0:T(8,128)(2,1)S(1)}, bf16[4,2,2,32,2560]{4,3,2,1,0:T(8,128)(2,1)}, u32[]{:S(2)}) copy-start(bf16[4,2,2,32,2560]{4,3,2,1,0:T(8,128)(2,1)} %copy-done.2) | copy-start | bytes 7864324
  120.1 5.0 %copy-start.10 = (bf16[864,2560]{1,0:T(8,128)(2,1)S(1)}, bf16[864,2560]{1,0:T(8,128)(2,1)}, u32[]{:S(2)}) copy-start(bf16[864,2560]{1,0:T(8,128)(2,1)} %get-tuple-element.23) | copy-start | bytes 13271044
  120.1 7.7 %slice-start = ((s8[4423680]{0:T(1024)(128)(4,1)}), s8[4194304]{0:T(1024)(128)(4,1)S(1)}, s32[]{:S(2)}) async-start(s8[4423680]{0:T(1024)(128)(4,1)} %bitcast.23), calls=%async_computation | async-start | bytes 8388608
  125.1 3.0 %slice-start.1 = ((s8[4423680]{0:T(1024)(128)(4,1)}), s8[229376]{0:T(1024)(128)(4,1)S(1)}, s32[]{:S(2)}) async-start(s8[4423680]{0:T(1024)(128)(4,1)} %bitcast.23), calls=%async_computation.1 | async-start | bytes 458752
